TPU v7x, 256 devices: a whole 4x4x8 slice. The times are simulated.
256 devices in a mesh: cfg: 2 (over x_lo), seq: 128 (over y, z, x_hi, core).
Axes of the slice: x: 4 (x_hi: 2, x_lo: 2; x = x_hi * 2 + x_lo), y: 4, z: 8, core: 2. Of those that a mesh axis runs over, the one named last changes fastest.
Arguments:
- coarse_hidden: bfloat16 [2, 256, 64, 2048], P('cfg', 'seq'), may hold values from -6 to 6
- coarse_modulation: float32 [2, 2, 2048], P('cfg'), may hold values from -3 to 3
- final_weight: bfloat16 [2048, 32], replicated, may hold values from -0.125 to 0.125
- coarse_latent: float32 [256, 2048], P('seq'), may hold values from -6 to 6
- step_index: int32 [1], replicated, may hold values from 0 to 49
- guide_index: int32 [1], replicated, may hold values from 0 to 4095
- guide_scales: float32 [4096], replicated, may hold values from 1.5 to 6
- upsample_weight: float32 [288, 32], replicated, may hold values from -0.375 to 0.375
- upsample_bias: float32 [32], replicated, may hold values from -3 to 3
- embed_weight: bfloat16 [32, 2048], replicated, may hold values from -1 to 1
- embed_bias: float32 [2048], replicated, may hold values from -3 to 3
- fine_modulation: float32 [3, 2048], replicated, may hold values from -3 to 3
- project_weight: bfloat16 [2048, 3072], P(('cfg', 'seq')), may hold values from -0.125 to 0.125
- query_gain: float32 [128], replicated, may hold values from 0.25 to 1.75
- key_gain: float32 [128], replicated, may hold values from 0.25 to 1.75
- text_keys: bfloat16 [256, 1024], replicated, may hold values from -6 to 6
- text_values: bfloat16 [256, 1024], replicated, may hold values from -6 to 6
- text_length: int32 [1], replicated, may hold values from 192 to 256
- output_weight: bfloat16 [1024, 2048], P(None, ('cfg', 'seq')), may hold values from -0.1875 to 0.1875
Outputs:
- guided_velocity: float32 [256, 2048], P('seq')
- fine_latent: float32 [256, 2, 4096], P('seq', 'cfg')
- fine_hidden: bfloat16 [256, 2, 128, 2048], P('seq', 'cfg')
All inputs are finite; a program needn't handle non-finite values.
Results may differ from a plain program's by a relative error of at most 0.0053.
Values may be sent and summed in bfloat16 or wider, within the bound.
A program may use at most 128 MiB of HBM per device.

v0:
```python
import jax
import jax.numpy as jnp
from jax import lax
from jax.sharding import PartitionSpec as P

HEADS = 8
STEPS = 50
epsilon = 1e-06
flow_shift = 5.0
highest = lax.Precision.HIGHEST


def from_partner(shard, axis, bit):
    return lax.ppermute(shard, axis, [(i, i ^ 1 << bit) for i in range(lax.axis_size(axis))])


def with_halo(block, sides, width):
    for axis, dim in sides:
        count = lax.axis_size(axis)
        forward = [(i, i + 1) for i in range(count - 1)]
        backward = [(target, source) for source, target in forward]
        low = lax.ppermute(
            lax.slice_in_dim(block, block.shape[dim] - width, None, axis=dim), axis, forward
        )
        high = lax.ppermute(lax.slice_in_dim(block, 0, width, axis=dim), axis, backward)
        block = jnp.concatenate([low, block, high], axis=dim)
    return block


def layer_norm(values):
    centred = values - jnp.mean(values, -1, keepdims=True)
    return centred * lax.rsqrt(jnp.mean(centred * centred, -1, keepdims=True) + epsilon)


def rms_heads(values, gain_vector, head_width):
    shaped = values.reshape(values.shape[0], -1, head_width)
    scaled = (
        shaped * lax.rsqrt(jnp.mean(shaped * shaped, -1, keepdims=True) + epsilon) * gain_vector
    )
    return scaled.reshape(values.shape[0], -1)


def sigma_at(step_value):
    fraction = 1.0 - step_value.astype(jnp.float32) / STEPS
    return flow_shift * fraction / (1.0 + (flow_shift - 1.0) * fraction)


def pick_scale(scale_table, slot_index):
    slots = jnp.arange(scale_table.shape[0], dtype=jnp.int32)
    return jnp.sum(jnp.where(slots == slot_index, scale_table, 0.0))


def attend(queries, image_keys, image_values, text_keys, text_values, image_mask, text_mask, heads):
    head_width = queries.shape[1] // heads
    score_scale = head_width ** (-0.5)
    dims = (((1,), (1,)), ((), ()))

    def one_head(head_index):
        column_start = head_index * head_width
        query_part = lax.dynamic_slice_in_dim(queries, column_start, head_width, 1)
        key_part = lax.dynamic_slice_in_dim(image_keys, column_start, head_width, 1)
        value_part = lax.dynamic_slice_in_dim(image_values, column_start, head_width, 1)
        text_key_part = lax.dynamic_slice_in_dim(text_keys, column_start, head_width, 1)
        text_value_part = lax.dynamic_slice_in_dim(text_values, column_start, head_width, 1)
        image_scores = (
            lax.dot_general(query_part, key_part, dims, preferred_element_type=jnp.float32)
            * score_scale
        )
        text_scores = (
            lax.dot_general(query_part, text_key_part, dims, preferred_element_type=jnp.float32)
            * score_scale
        )
        image_weights = jnp.where(image_mask, jnp.exp(image_scores), 0.0)
        text_weights = jnp.where(text_mask, jnp.exp(text_scores), 0.0)
        denominator = jnp.sum(image_weights, 1, keepdims=True) + jnp.sum(
            text_weights, 1, keepdims=True
        )
        image_weights = (image_weights / denominator).astype(jnp.bfloat16)
        text_weights = (text_weights / denominator).astype(jnp.bfloat16)
        return jnp.dot(image_weights, value_part, preferred_element_type=jnp.float32) + jnp.dot(
            text_weights, text_value_part, preferred_element_type=jnp.float32
        )

    stacked = lax.map(one_head, jnp.arange(heads, dtype=jnp.int32))
    return stacked.transpose(1, 0, 2).reshape(queries.shape[0], -1).astype(jnp.bfloat16)


def conv_rows(above, centre, below, upsample_weight, upsample_bias):
    tap_list = []
    for row_set in (above, centre, below):
        breadth = row_set.shape[1]
        padded = jnp.pad(row_set, ((0, 0), (1, 1), (0, 0)))
        for col_shift in range(3):
            tap_list.append(padded[:, col_shift : col_shift + breadth])
    patches = jnp.concatenate(tap_list, -1)
    flat_patches = patches.reshape(-1, patches.shape[-1])
    product = jnp.dot(flat_patches, upsample_weight, precision=highest).reshape(centre.shape)
    return product + upsample_bias + centre


def per_device(
    coarse_hidden,
    coarse_modulation,
    final_weight,
    coarse_latent,
    step_index,
    guide_index,
    guide_scales,
    upsample_weight,
    upsample_bias,
    embed_weight,
    embed_bias,
    fine_modulation,
    project_weight,
    query_gain,
    key_gain,
    text_keys,
    text_values,
    text_length,
    output_weight,
):
    row_count = coarse_hidden.shape[1]
    row_cells = coarse_hidden.shape[2]
    model_width = coarse_hidden.shape[3]
    channels = final_weight.shape[1]
    head_width = query_gain.shape[0]
    inner = project_weight.shape[1] // 3
    reach = max(row_count // 2, 1)
    branch = lax.axis_index("cfg")
    seq_index = lax.axis_index("seq")
    normed = layer_norm(coarse_hidden[0].astype(jnp.float32))
    modulated = (normed * (1.0 + coarse_modulation[0, 1]) + coarse_modulation[0, 0]).astype(
        jnp.bfloat16
    )
    velocity = jnp.dot(
        modulated.reshape(row_count * row_cells, model_width),
        final_weight,
        preferred_element_type=jnp.float32,
    ).reshape(row_count, row_cells * channels)
    partner = from_partner(velocity, "cfg", 0)
    conditional = jnp.where(branch == 0, velocity, partner)
    unconditional = jnp.where(branch == 0, partner, velocity)
    guidance = pick_scale(guide_scales, guide_index[0])
    guided = unconditional + guidance * (conditional - unconditional)
    stepped = coarse_latent + (sigma_at(step_index[0] + 1) - sigma_at(step_index[0])) * guided
    scale = 1.0 + fine_modulation[1]
    embed32 = embed_weight.astype(jnp.float32)
    embed_centred = embed32 - jnp.mean(embed32, -1, keepdims=True)
    bias_centred = embed_bias - jnp.mean(embed_bias)
    folded_left = jnp.concatenate(
        [embed_centred * scale, (bias_centred * scale)[None], fine_modulation[0][None]], 0
    )
    depth = project_weight.shape[0]
    device = branch * lax.axis_size("seq") + seq_index
    left_part = lax.dynamic_slice_in_dim(folded_left, device * depth, depth, 1)
    folded = lax.psum(
        jnp.dot(left_part, project_weight.astype(jnp.float32), precision=highest), ("cfg", "seq")
    )
    output_rows = lax.all_gather(output_weight.T, ("cfg", "seq"), axis=0, tiled=True)

    def embed_rows(grid_rows):
        grid_tokens = grid_rows.reshape(-1, channels).astype(jnp.bfloat16)
        centred = (
            jnp.dot(grid_tokens.astype(jnp.float32), embed_centred, precision=highest)
            + bias_centred
        )
        rstd = lax.rsqrt(jnp.mean(centred * centred, -1, keepdims=True) + epsilon)
        return (grid_tokens, rstd)

    def project(tokens_rstd, start, stop):
        tokens, rstd = tokens_rstd
        part = folded[:, start:stop]
        product = jnp.dot(tokens.astype(jnp.float32), part[:channels], precision=highest)
        return rstd * (product + part[channels]) + part[channels + 1]

    latent_grid = stepped.reshape(row_count, row_cells, channels)
    rim_width = reach + 1
    rimmed = with_halo(latent_grid, (("seq", 0),), rim_width)
    upsampled = jnp.repeat(jnp.repeat(rimmed, 2, 0), 2, 1)
    span = row_count + 2 * reach
    wide_grid = conv_rows(
        upsampled[1 : 1 + 2 * span],
        upsampled[2 : 2 + 2 * span],
        upsampled[3 : 3 + 2 * span],
        upsample_weight,
        upsample_bias,
    )
    grouped = wide_grid.reshape(span, 2, 2 * row_cells, channels)
    fine_grid = lax.dynamic_index_in_dim(
        grouped[reach : reach + row_count], branch, 1, keepdims=False
    )
    own = embed_rows(fine_grid)
    fine_state = jnp.dot(own[0], embed_weight, preferred_element_type=jnp.float32) + embed_bias
    around = embed_rows(wide_grid)
    token_count = own[0].shape[0]
    query_sum = project(own, 0, inner)
    key_sum = project(around, inner, 2 * inner)
    value_sum = project(around, 2 * inner, 3 * inner)
    queries = rms_heads(query_sum, query_gain, head_width).astype(jnp.bfloat16)
    keys = rms_heads(key_sum, key_gain, head_width).astype(jnp.bfloat16)
    values = value_sum.astype(jnp.bfloat16)
    image_keys, image_values = (keys, values)
    normed_text_keys = rms_heads(text_keys.astype(jnp.float32), key_gain, head_width).astype(
        jnp.bfloat16
    )
    key_count = image_keys.shape[0]
    query_rows = jnp.arange(token_count, dtype=jnp.int32) // (2 * row_cells)
    key_rows = jnp.arange(key_count, dtype=jnp.int32) // (4 * row_cells)
    distance = key_rows[None, :] - query_rows[:, None]
    global_rows = seq_index * row_count + key_rows - reach
    row_valid = (global_rows >= 0) & (global_rows < row_count * lax.axis_size("seq"))
    image_mask = (distance >= 0) & (distance <= 2 * reach) & row_valid[None, :]
    text_mask = (jnp.arange(text_keys.shape[0], dtype=jnp.int32) < text_length[0])[None, :]
    attended = attend(
        queries,
        image_keys,
        image_values,
        normed_text_keys,
        text_values,
        image_mask,
        text_mask,
        HEADS,
    )
    output_part = lax.dot_general(
        attended, output_rows, (((1,), (1,)), ((), ())), preferred_element_type=jnp.float32
    )
    fine_hidden = (fine_state + fine_modulation[2] * output_part).astype(jnp.bfloat16)
    fine_hidden = fine_hidden.reshape(row_count, 1, 2 * row_cells, model_width)
    fine_latent = fine_grid.reshape(row_count, 1, 2 * row_cells * channels)
    return (guided, fine_latent, fine_hidden)


def solution(mesh):
    placed = (
        P("cfg", "seq", None, None),
        P("cfg", None, None),
        P(),
        P("seq", None),
        P(),
        P(),
        P(),
        P(),
        P(),
        P(),
        P(),
        P(),
        P(("cfg", "seq"), None),
        P(),
        P(),
        P(),
        P(),
        P(),
        P(None, ("cfg", "seq")),
    )
    return jax.shard_map(
        per_device,
        mesh=mesh,
        in_specs=placed,
        out_specs=(P("seq", None), P("seq", "cfg", None), P("seq", "cfg", None, None)),
        check_vma=False,
    )
```

profile of v0, /device:TPU:32, one launch (start us, length us, event | category | flops | bytes accessed | tf_op | source)
XLA Modules:
  0.0 696.4 jit_solution(8204464123050728577)
XLA Ops:
  7.3 1.5 fusion.84
  8.7 1.0 convert_reduce_fusion.1
  9.8 1.0 fusion.43
  10.8 1.3 reduce_sum.112
  12.7 0.7 fusion.79
  13.5 2.0 fusion.65
  17.0 1.6 collective-permute-start
  23.5 1.3 multiply_add_fusion.1
  24.9 1.9 collective-permute-start.1
  27.4 6.0 collective-permute-start.2
  33.5 1.8 collective-permute-done.2
  37.4 0.9 fusion.31
  38.5 0.7 reshape.247
  39.3 1.2 fusion.28
  40.4 4.5 multiply_reduce_fusion
  45.0 223.4 %all-reduce.5.cloned.1.call-done = f32[34,3072]{1,0:T(8,128)} async-done(((f32[34,3072]{1,0:T(8,128)}), f32[34,3072]{1,0:T(8,128)}) %all-reduce.5.cloned.1.call-update) | async-done | bytes 417808 | tf_op jit(solution)/shard_map/psum | solution.py:156
  268.4 0.9 fusion.82
  269.3 1.6 fusion.30
  271.7 3.4 bitcast_reduce_fusion
  275.9 1.1 fusion.23
  277.0 4.4 add_convert_fusion
  281.9 58.2 %while.11 = (s32[]{:T(128)}, bf16[8,256,128]{1,2,0:T(8,128)(2,1)}, s32[8]{0:T(128)}, bf16[256,1024]{1,0:T(8,128)(2,1)S(1)}, bf16[1024,1024]{0,1:T(8,128)(2,1)S(1...) while((s32[]{:T(128)}, bf16[8,256,128]{1,2,0:T(8,128)(2,1)}, ...), condition=%wide.region_14.15_spmd.clone, body=%wide.region_11.14_spmd.clone.sunk | while | flops 170786816 | bytes 4014055 | solution.py:84
  281.9 1.2 dynamic_slice.86
  283.8 0.7 compare_reduce_fusion.2
  284.7 1.3 fusion.102
  286.0 1.1 fusion.103
  287.1 1.3 fusion.104
  289.2 1.2 dynamic_slice.86
  291.0 0.7 compare_reduce_fusion.2
  291.9 1.3 fusion.102
  293.3 1.1 fusion.103
  294.3 1.3 fusion.104
  296.4 1.2 dynamic_slice.86
  298.3 0.7 compare_reduce_fusion.2
  299.2 1.3 fusion.102
  300.5 1.1 fusion.103
  301.6 1.3 fusion.104
  303.7 1.2 dynamic_slice.86
  305.6 0.7 compare_reduce_fusion.2
  306.5 1.3 fusion.102
  307.8 1.1 fusion.103
  308.9 1.3 fusion.104
  311.0 1.2 dynamic_slice.86
  312.9 0.7 compare_reduce_fusion.2
  313.8 1.3 fusion.102
  315.1 1.1 fusion.103
  316.2 1.3 fusion.104
  318.3 1.2 dynamic_slice.86
  321.0 1.3 fusion.102
  322.4 1.1 fusion.103
  323.4 1.3 fusion.104
  325.5 1.2 dynamic_slice.86
  327.4 0.7 compare_reduce_fusion.2
  328.3 1.3 fusion.102
  329.6 1.1 fusion.103
  330.7 1.3 fusion.104
  332.8 1.2 dynamic_slice.86
  334.7 0.7 compare_reduce_fusion.2
  335.6 1.3 fusion.102
  336.9 1.1 fusion.103
  338.0 1.3 fusion.104
  340.1 344.3 %all-gather.2.cloned.1.call-done = bf16[2048,1024]{1,0:T(8,128)(2,1)} async-done(((bf16[8,1024]{1,0:T(8,128)(2,1)}), bf16[2048,1024]{1,0:T(8,128)(2,1)}) %all-gather.2.cloned.1.call-update) | async-done | bytes 4194320 | tf_op jit(solution)/shard_map/all_gather | solution.py:159
  684.4 3.6 convolution_multiply_fusion.2
  688.1 1.4 fusion.27
  (137 shorter events, 18.4 us)
Async XLA Ops:
  7.2 9.5 %copy-start = (bf16[2048,32]{0,1:T(8,128)(2,1)S(1)}, bf16[2048,32]{0,1:T(8,128)(2,1)}, u32[]{:S(2)}) copy-start(bf16[2048,32]{0,1:T(8,128)(2,1)} %param.23) | copy-start | bytes 393220
  7.2 8.4 %copy-start.1 = (bf16[1,2,64,2048]{3,2,1,0:T(8,128)(2,1)S(1)}, bf16[1,2,64,2048]{3,2,1,0:T(8,128)(2,1)}, u32[]{:S(2)}) copy-start(bf16[1,2,64,2048]{3,2,1,0:T(8,128)(2,1)} %param.21) | copy-start | bytes 1572868
  7.2 8.9 %copy-start.8 = (f32[1,2,2048]{2,1,0:T(2,128)S(1)}, f32[1,2,2048]{2,1,0:T(2,128)}, u32[]{:S(2)}) copy-start(f32[1,2,2048]{2,1,0:T(2,128)} %param.22) | copy-start | bytes 49156
  7.2 261.2 %all-reduce.5.cloned.1.call-start = ((), (), s32[]{:S(2)}) async-start(), calls=%async_computation | async-start | bytes 983040 | tf_op jit(solution)/shard_map/psum | solution.py:156
  13.4 6.4 copy-start.12
  13.5 6.5 copy-start.13
  13.5 6.5 copy-start.2
  15.5 668.9 %all-gather.2.cloned.1.call-start = ((), (), s32[]{:S(2)}) async-start(), calls=%async_computation.1 | async-start | bytes 4210688 | tf_op jit(solution)/shard_map/all_gather | solution.py:159
  17.0 6.4 collective-permute-start
  20.1 0.8 copy-start.9
  20.6 2.9 copy-start.10
  24.9 8.6 %collective-permute-start.1 = (f32[2,64,32]{2,1,0:T(8,128)S(1)}, f32[2,64,32]{2,1,0:T(8,128)S(1)}, u32[]{:S(2)}, u32[]{:S(2)}) collective-permute-start(f32[2,64,32]{2,1,0:T(8,128)S(1)} %reshape.230), channel_id=1, source_target_pairs={{0,1},{1,2},{2,3},{3,4},{4,5},{5,6},{6,7},{7,8},{8,9},{9,10},{10,1... | collective-permute-start | bytes 49160 | tf_op jit(solution)/shard_map/ppermute | solution.py:22
  27.4 7.9 %collective-permute-start.2 = (f32[2,64,32]{2,1,0:T(8,128)S(1)}, f32[2,64,32]{2,1,0:T(8,128)S(1)}, u32[]{:S(2)}, u32[]{:S(2)}) collective-permute-start(f32[2,64,32]{2,1,0:T(8,128)S(1)} %reshape.230), channel_id=1, source_target_pairs={{1,0},{2,1},{3,2},{4,3},{5,4},{6,5},{7,6},{8,7},{9,8},{10,9},{11,1... | collective-permute-start | bytes 49160 | tf_op jit(solution)/shard_map/ppermute | solution.py:25
  36.3 1.1 copy-start.7
  36.3 1.1 copy-start.11
  36.9 2.3 copy-start.3
  38.4 233.4 %copy-start.5 = (bf16[8,4,8,128]{3,2,1,0:T(8,128)(2,1)}, bf16[8,4,8,128]{3,2,1,0:T(8,128)(2,1)S(1)}, u32[]{:S(2)}) copy-start(bf16[8,4,8,128]{3,2,1,0:T(8,128)(2,1)S(1)} %convert_bitcast_fusion) | copy-start | bytes 196612
  275.9 1.1 copy-start.6
  684.4 3.6 copy-start.4
Sparse Core Ops, SparseCore 0:
  15.6 252.6 all-reduce.4
  270.3 414.1 all-gather.1
where the time goes:
time: 698 us; the launch traced here: 696 us
  waiting for transfers between devices  570 us (82%)
  matrix products  55 us (8%)
  local copies, waits for them, and re-layouts  21.8 us (3%)
  other arithmetic  18.2 us (3%)
  between operations  16.7 us (2%)
  starting transfers between devices  9.61 us (1%)
    all_gather x1, waiting for transfers between devices, per_device(): lax.all_gather(output_weight.T, ('cfg', 'seq'), axis=0, tiled=True)  344 us
    psum x1, waiting for transfers between devices, per_device(): lax.psum(jnp.dot(left_part, project_weight.astype(jnp.float32), precision...  223 us
  transfers between devices with their start and end apart: 5, of which 3 were waited for; matrix products, arithmetic and copies ran while one was open for 12% of the time, Pallas kernels for 0%

commit v1 on v0

--- a/solution.py
+++ b/solution.py
@@ -156,7 +156,12 @@
     folded = lax.psum(
         jnp.dot(left_part, project_weight.astype(jnp.float32), precision=highest), ("cfg", "seq")
     )
-    output_rows = lax.all_gather(output_weight.T, ("cfg", "seq"), axis=0, tiled=True)
+    output_rows = jnp.concatenate(
+        lax.all_to_all(
+            jnp.stack([output_weight.T] * lax.axis_size(("cfg", "seq"))), ("cfg", "seq"), 0, 0
+        ),
+        axis=0,
+    )
 
     def embed_rows(grid_rows):
         grid_tokens = grid_rows.reshape(-1, channels).astype(jnp.bfloat16)

time: 698 us -> 376 us (0.54)
  waiting for transfers between devices: 570 us -> 229 us
  starting transfers between devices: 9.61 us -> 24.7 us
    all_gather x1 -> x0, waiting for transfers between devices: 344 us -> none  [per_device(): lax.all_gather(output_weight.T, ('cfg', 'seq'), axis=0, tiled=True)]
    ppermute x1, waiting for transfers between devices: 0.01 us -> 75.9 us  [with_halo(): lax.ppermute(lax.slice_in_dim(block, block.shape[dim] - width, None, axis...]
    psum x1, waiting for transfers between devices: 223 us -> 153 us  [per_device(): lax.psum(jnp.dot(left_part, project_weight.astype(jnp.float32), precision...]
    all_to_all x0 -> x1, starting transfers between devices: none -> 15.1 us  [per_device(): lax.all_to_all(jnp.stack([output_weight.T] * lax.axis_size(('cfg', 'seq')...]
  transfers between devices with their start and end apart: 5 -> 5, of which waited for: 3 -> 2; matrix products, arithmetic and copies ran while one was open for 12% -> 23% of each run, Pallas kernels for 0% -> 0%
where the time goes in v1:
time: 376 us; the launch traced here: 371 us
  waiting for transfers between devices  229 us (61%)
  matrix products  54.4 us (14%)
  starting transfers between devices  24.7 us (7%)
  local copies, waits for them, and re-layouts  24.3 us (6%)
  other arithmetic  18 us (5%)
  between operations  16.7 us (4%)
  loops' own time  4.72 us (1%)
    psum x1, waiting for transfers between devices, per_device(): lax.psum(jnp.dot(left_part, project_weight.astype(jnp.float32), precision...  153 us
    ppermute x1, waiting for transfers between devices, with_halo(): lax.ppermute(lax.slice_in_dim(block, block.shape[dim] - width, None, axis...  75.9 us
    all_to_all x1, starting transfers between devices, per_device(): lax.all_to_all(jnp.stack([output_weight.T] * lax.axis_size(('cfg', 'seq')...  15.1 us
    dot_general x8, matrix products, one_head(): jnp.dot(image_weights, value_part, preferred_element_type=jnp.float32)  10.6 us
    dot_general x8, matrix products, one_head(): lax.dot_general(query_part, key_part, dims, preferred_element_type=jnp.fl...  10.6 us
    dynamic_slice x8, local copies, waits for them, and re-layouts, attend(): stacked = lax.map(one_head, jnp.arange(heads, dtype=jnp.int32))  9.71 us
    dot_general x3, matrix products, project(): jnp.dot(tokens.astype(jnp.float32), part[:channels], precision=highest)  9.45 us
    dot_general x8, matrix products, one_head(): jnp.dot(text_weights, text_value_part, preferred_element_type=jnp.float32)  8.64 us
  transfers between devices with their start and end apart: 5, of which 2 were waited for; matrix products, arithmetic and copies ran while one was open for 23% of the time, Pallas kernels for 0%

profile of v1, /device:TPU:32, one launch (start us, length us, event | category | flops | bytes accessed | tf_op | source)
XLA Modules:
  0.0 371.4 jit_solution(17636255506332269571)
XLA Ops:
  7.3 1.3 convert_reduce_fusion
  8.6 1.3 fusion.43
  10.0 0.8 slice_add_fusion.1
  10.9 1.4 fusion.47
  12.7 1.6 collective-permute-start
  16.5 1.3 fusion.70
  17.7 2.5 stack.2
  20.3 15.1 %all-to-all-start = ((bf16[256,8,1024]{2,1,0:T(8,128)(2,1)}), bf16[256,8,1024]{2,1,0:T(8,128)(2,1)}, u32[]{:S(2)}, u32[]{:S(2)}) async-start(bf16[256,8,1024]{2,1,0:T(8,128)(2,1)} %stack.2), calls=%async_computation | async-start | bytes 8388608 | tf_op jit(solution)/shard_map/all_to_all | solution.py:160
  40.1 1.3 multiply_add_fusion.1
  41.5 2.1 collective-permute-start.1
  44.1 5.9 %collective-permute-start.2 = (f32[2,64,32]{2,1,0:T(8,128)S(1)}, f32[2,64,32]{2,1,0:T(8,128)S(1)}, u32[]{:S(2)}, u32[]{:S(2)}) collective-permute-start(f32[2,64,32]{2,1,0:T(8,128)S(1)} %reshape.235), channel_id=1, source_target_pairs={{1,0},{2,1},{3,2},{4,3},{5,4},{6,5},{7,6},{8,7},{9,8},{10,9},{11,1... | collective-permute-start | bytes 49160 | tf_op jit(solution)/shard_map/ppermute | solution.py:25
  50.0 75.9 %collective-permute-done.1 = f32[2,64,32]{2,1,0:T(8,128)S(1)} collective-permute-done((f32[2,64,32]{2,1,0:T(8,128)S(1)}, f32[2,64,32]{2,1,0:T(8,128)S(1)}, u32[]{:S(2)}, u32[]{:S(2)}) %collective-permute-start.1) | collective-permute-done | bytes 16416 | tf_op jit(solution)/shard_map/ppermute | solution.py:22
  128.1 0.9 fusion.36
  129.1 0.7 reshape.253
  129.9 1.2 fusion.33
  131.0 4.5 %multiply_reduce_fusion = f32[1024]{0:T(1024)S(1)} fusion(f32[2048]{0:T(1024)S(1)} %get-tuple-element.189, bf16[32,2048]{1,0:T(8,128)(2,1)S(1)} %copy-done.2, f32[32]{0:T(128)S(1)} %broadcast_multiply_fusion.1, bf16[8,4,8,128]{3,2,1,0:T(8,128)(2,1)S(1)} %convert_bitcast_fusion), kind=kOutput, calls=%fused_computation.29 | convolution fusion | flops 811727872 | bytes 209024 | tf_op jit(solution)/shard_map/dot_general | solution.py:169
  135.6 152.7 %all-reduce.5.cloned.1.call-done = f32[34,3072]{1,0:T(8,128)} async-done(((f32[34,3072]{1,0:T(8,128)}), f32[34,3072]{1,0:T(8,128)}) %all-reduce.5.cloned.1.call-update) | async-done | bytes 417808 | tf_op jit(solution)/shard_map/psum | solution.py:156
  288.3 0.9 fusion.87
  289.2 1.6 fusion.35
  291.6 3.4 bitcast_reduce_fusion
  295.8 1.1 fusion.25
  296.9 4.4 %add_convert_fusion = bf16[1024,1024]{0,1:T(8,128)(2,1)} fusion(f32[1024]{0:T(1024)S(1)} %bitcast.147, f32[1024]{0:T(1024)S(1)} %bitcast.146, f32[1024]{0:T(1024)S(1)} %add_rsqrt_fusion.3, f32[34,3072]{1,0:T(8,128)} %all-reduce.5.cloned.1.call-done, bf16[8,4,8,128]{3,2,1,0:T(8,128)(2,1)S(1)} %copy-done.6), kind=kOutput, calls=%fused_computation.36 | convolution fusion | flops 406847488 | bytes 2306048 | tf_op jit(solution)/shard_map/dot_general | solution.py:178
  301.9 57.6 %while.11 = (s32[]{:T(128)}, bf16[8,256,128]{1,2,0:T(8,128)(2,1)}, s32[8]{0:T(128)}, bf16[256,1024]{1,0:T(8,128)(2,1)S(1)}, bf16[1024,1024]{0,1:T(8,128)(2,1)S(1...) while((s32[]{:T(128)}, bf16[8,256,128]{1,2,0:T(8,128)(2,1)}, ...), condition=%wide.region_14.15_spmd.clone, body=%wide.region_11.14_spmd.clone.sunk | while | flops 170786816 | bytes 4014055 | solution.py:84
  301.9 1.2 dynamic_slice.86
  303.7 0.7 compare_reduce_fusion.2
  304.6 1.3 fusion.106
  305.9 1.1 fusion.107
  307.0 1.3 fusion.108
  309.1 1.2 dynamic_slice.86
  310.9 0.7 compare_reduce_fusion.2
  311.8 1.3 fusion.106
  313.1 1.1 fusion.107
  314.2 1.3 fusion.108
  316.3 1.2 dynamic_slice.86
  318.1 0.7 compare_reduce_fusion.2
  319.0 1.3 fusion.106
  320.3 1.1 fusion.107
  321.4 1.3 fusion.108
  323.5 1.2 dynamic_slice.86
  325.3 0.7 compare_reduce_fusion.2
  326.2 1.3 fusion.106
  327.5 1.1 fusion.107
  328.6 1.3 fusion.108
  330.7 1.2 dynamic_slice.86
  332.5 0.7 compare_reduce_fusion.2
  333.4 1.3 fusion.106
  334.7 1.1 fusion.107
  335.8 1.3 fusion.108
  337.9 1.2 dynamic_slice.86
  340.6 1.3 fusion.106
  341.9 1.1 fusion.107
  343.0 1.3 fusion.108
  345.1 1.2 dynamic_slice.86
  346.9 0.7 compare_reduce_fusion.2
  347.8 1.3 fusion.106
  349.1 1.1 fusion.107
  350.2 1.3 fusion.108
  352.3 1.2 dynamic_slice.86
  354.1 0.7 compare_reduce_fusion.2
  355.0 1.3 fusion.106
  356.3 1.1 fusion.107
  357.4 1.3 fusion.108
  359.5 3.6 fusion.27
  363.1 1.4 fusion.32
  (141 shorter events, 18.8 us)
Async XLA Ops:
  7.2 5.2 %copy-start = (bf16[2048,32]{0,1:T(8,128)(2,1)S(1)}, bf16[2048,32]{0,1:T(8,128)(2,1)}, u32[]{:S(2)}) copy-start(bf16[2048,32]{0,1:T(8,128)(2,1)} %param.23) | copy-start | bytes 393220
  7.2 7.1 %copy-start.9 = (f32[3,2048]{1,0:T(4,128)S(1)}, f32[3,2048]{1,0:T(4,128)}, u32[]{:S(2)}) copy-start(f32[3,2048]{1,0:T(4,128)} %param.32) | copy-start | bytes 73732
  7.2 7.7 %copy-start.2 = (bf16[32,2048]{1,0:T(8,128)(2,1)S(1)}, bf16[32,2048]{1,0:T(8,128)(2,1)}, u32[]{:S(2)}) copy-start(bf16[32,2048]{1,0:T(8,128)(2,1)} %param.30) | copy-start | bytes 393220
  7.2 8.0 %copy-start.3 = (f32[2048]{0:T(1024)S(1)}, f32[2048]{0:T(1024)}, u32[]{:S(2)}) copy-start(f32[2048]{0:T(1024)} %param.31) | copy-start | bytes 24580
  7.2 9.2 %copy-start.8 = (bf16[8,3072]{1,0:T(8,128)(2,1)S(1)}, bf16[8,3072]{1,0:T(8,128)(2,1)}, u32[]{:S(2)}) copy-start(bf16[8,3072]{1,0:T(8,128)(2,1)} %param.33) | copy-start | bytes 147460
  7.2 281.1 %all-reduce.5.cloned.1.call-start = ((), (), s32[]{:S(2)}) async-start(), calls=%async_computation.1 | async-start | bytes 983040 | tf_op jit(solution)/shard_map/psum | solution.py:156
  8.6 9.2 %copy-start.10 = (bf16[1024,8]{0,1:T(8,128)(2,1)S(1)}, bf16[1024,8]{0,1:T(8,128)(2,1)}, u32[]{:S(2)}) copy-start(bf16[1024,8]{0,1:T(8,128)(2,1)} %param.39) | copy-start | bytes 49156
  12.7 27.4 %collective-permute-start = (f32[2,2048]{1,0:T(2,128)S(1)}, f32[2,2048]{1,0:T(2,128)S(1)}, u32[]{:S(2)}, u32[]{:S(2)}) collective-permute-start(f32[2,2048]{1,0:T(2,128)S(1)} %reshape.234), channel_id=1, source_target_pairs={{0,128},{128,0},{1,129},{129,1},{2,130},{130,2},{3,131},{131,3},{4... | collective-permute-start | bytes 49160 | tf_op jit(solution)/shard_map/ppermute | solution.py:14
  20.2 16.4 %copy-start.14 = (f32[128]{0:T(128)S(1)}, f32[128]{0:T(128)}, u32[]{:S(2)}) copy-start(f32[128]{0:T(128)} %param.34) | copy-start | bytes 1540
  20.2 16.4 %copy-start.15 = (f32[128]{0:T(128)S(1)}, f32[128]{0:T(128)}, u32[]{:S(2)}) copy-start(f32[128]{0:T(128)} %param.35) | copy-start | bytes 1540
  20.2 16.4 %copy-start.1 = (bf16[256,1024]{1,0:T(8,128)(2,1)S(1)}, bf16[256,1024]{1,0:T(8,128)(2,1)}, u32[]{:S(2)}) copy-start(bf16[256,1024]{1,0:T(8,128)(2,1)} %param.36) | copy-start | bytes 1572868
  20.3 339.2 %all-to-all-start = ((bf16[256,8,1024]{2,1,0:T(8,128)(2,1)}), bf16[256,8,1024]{2,1,0:T(8,128)(2,1)}, u32[]{:S(2)}, u32[]{:S(2)}) async-start(bf16[256,8,1024]{2,1,0:T(8,128)(2,1)} %stack.2), calls=%async_computation | async-start | bytes 8388608 | tf_op jit(solution)/shard_map/all_to_all | solution.py:160
  36.8 0.8 copy-start.11
  37.3 2.8 copy-start.12
  41.5 84.4 %collective-permute-start.1 = (f32[2,64,32]{2,1,0:T(8,128)S(1)}, f32[2,64,32]{2,1,0:T(8,128)S(1)}, u32[]{:S(2)}, u32[]{:S(2)}) collective-permute-start(f32[2,64,32]{2,1,0:T(8,128)S(1)} %reshape.235), channel_id=1, source_target_pairs={{0,1},{1,2},{2,3},{3,4},{4,5},{5,6},{6,7},{7,8},{8,9},{9,10},{10,1... | collective-permute-start | bytes 49160 | tf_op jit(solution)/shard_map/ppermute | solution.py:22
  44.1 81.8 %collective-permute-start.2 = (f32[2,64,32]{2,1,0:T(8,128)S(1)}, f32[2,64,32]{2,1,0:T(8,128)S(1)}, u32[]{:S(2)}, u32[]{:S(2)}) collective-permute-start(f32[2,64,32]{2,1,0:T(8,128)S(1)} %reshape.235), channel_id=1, source_target_pairs={{1,0},{2,1},{3,2},{4,3},{5,4},{6,5},{7,6},{8,7},{9,8},{10,9},{11,1... | collective-permute-start | bytes 49160 | tf_op jit(solution)/shard_map/ppermute | solution.py:25
  126.9 1.1 copy-start.7
  126.9 1.1 copy-start.13
  129.0 162.7 %copy-start.5 = (bf16[8,4,8,128]{3,2,1,0:T(8,128)(2,1)}, bf16[8,4,8,128]{3,2,1,0:T(8,128)(2,1)S(1)}, u32[]{:S(2)}) copy-start(bf16[8,4,8,128]{3,2,1,0:T(8,128)(2,1)S(1)} %convert_bitcast_fusion) | copy-start | bytes 196612
  295.8 1.1 copy-start.6
  359.5 3.6 copy-start.4
Sparse Core Ops, SparseCore 0:
  17.9 270.3 all-reduce.4
